TPU v7x, 1024 devices: a whole 4x4x32 slice. The times are simulated.
1024 devices in a mesh: dp: 32 (over z), expert: 4 (over x_lo, core), tensor: 8 (over y, x_hi).
Axes of the slice: x: 4 (x_hi: 2, x_lo: 2; x = x_hi * 2 + x_lo), y: 4, z: 32, core: 2. Of those that a mesh axis runs over, the one named last changes fastest.
Arguments:
- tokens: bfloat16 [256, 6144], P('dp'), may hold values from -6 to 6
- expert_ids: int32 [256, 2], P('dp'), may hold values from 0 to 3, all different within a row; in each aligned block of 8 rows (0 to 7, 8 to 15, ...) at most 5 rows name the same one
- gates: float32 [256, 2], P('dp'), may hold values from 0.1 to 1
- w_gate: bfloat16 [4, 8192, 6144], P('expert', 'tensor', 'dp'), may hold values from -0.078125 to 0.078125
- w_up: bfloat16 [4, 8192, 6144], P('expert', 'tensor', 'dp'), may hold values from -0.078125 to 0.078125
- w_out: bfloat16 [4, 8192, 6144], P('expert', 'tensor', 'dp'), may hold values from -0.0625 to 0.0625
- cotangent: bfloat16 [256, 6144], P('dp'), may hold values from -6 to 6
Outputs:
- mixed: bfloat16 [256, 6144], P('dp', ('expert', 'tensor'))
- d_tokens: bfloat16 [256, 6144], P('dp', ('expert', 'tensor'))
- d_gate: bfloat16 [4, 8192, 6144], P('expert', 'tensor', 'dp')
- d_up: bfloat16 [4, 8192, 6144], P('expert', 'tensor', 'dp')
- d_out: bfloat16 [4, 8192, 6144], P('expert', 'tensor', 'dp')
Inputs may be any that keep to these rules, and one draw needn't show every extreme that they name: `expert_ids`: each token names two different experts. Among the 8 tokens of one dp index no expert is named more than 5 times, a bound that some block reaches.
All inputs are finite; a program needn't handle non-finite values.
Results may differ from a plain program's by a relative error of at most 0.0057.
Values may be sent and summed in bfloat16 or wider, within the bound.
A program may use at most 32 MiB of HBM per device.

v0:
```python
import jax
import jax.numpy as jnp
from jax import lax
from jax.sharding import PartitionSpec as P


def shortened(x):

    def short(part):
        return part.astype(jnp.bfloat16) if part.dtype == jnp.float32 else part

    return jax.tree.map(short, x)


def routing(expert_ids, gates, expert_id, capacity):
    group = expert_ids.shape[0]
    flat = expert_ids.reshape(group * 2)
    mine = (flat == expert_id).astype(jnp.int32)
    earlier = jnp.cumsum(mine) - mine
    cap_ids = jnp.arange(capacity, dtype=jnp.int32)
    hits = ((earlier[None, :] == cap_ids[:, None]) & (mine[None, :] == 1)).astype(jnp.float32)
    picks = hits.reshape(capacity, group, 2).sum(axis=2)
    weighted = (hits * gates.reshape(group * 2)[None, :]).reshape(capacity, group, 2).sum(axis=2)
    return (picks, weighted)


def rows_in(parts):
    return (lax.all_to_all(parts[0], "dp", split_axis=1, concat_axis=0, tiled=True),)


def reduce_acts(parts):
    return lax.psum_scatter(parts, "dp", scatter_dimension=0, tiled=True)


def collect(parts):
    return jax.tree.map(
        lambda part, own: part.astype(own.dtype),
        lax.all_gather(shortened(parts), "dp", axis=0, tiled=True),
        parts,
    )


def results_back(parts):
    return (lax.all_to_all(parts[0], "dp", split_axis=0, concat_axis=1, tiled=True),)


def token_sums(parts):
    return (lax.psum_scatter(parts[0], ("expert", "tensor"), scatter_dimension=1, tiled=True),)


def project_cols(left, right):
    return lax.dot_general(
        left, right, (((1,), (1,)), ((), ())), preferred_element_type=jnp.float32
    )


def project_rows(left, right):
    return lax.dot_general(
        left, right, (((0,), (0,)), ((), ())), preferred_element_type=jnp.float32
    )


def combine(table, returned):
    return lax.dot_general(
        table, returned, (((0,), (0,)), ((), ())), precision=lax.Precision.HIGHEST
    )


def swiglu(gate_share, up_share):
    active = jax.nn.silu(gate_share)
    return (active, (active * up_share).astype(jnp.bfloat16))


def swiglu_grad(gate_share, up_share, active, dh_share):
    sig = jax.nn.sigmoid(gate_share)
    grad_gate = (dh_share * up_share * (sig * (1.0 + gate_share * (1.0 - sig)))).astype(
        jnp.bfloat16
    )
    grad_up = (dh_share * active).astype(jnp.bfloat16)
    return (grad_gate, grad_up)


def per_device(tokens, expert_ids, gates, w_gate, w_up, w_out, cotangent):
    highest = lax.Precision.HIGHEST
    expert_id = lax.axis_index("expert")
    group = tokens.shape[0]
    capacity = 2 * (group // lax.axis_size("expert")) + 1
    picks, weighted = routing(expert_ids, gates, expert_id, capacity)
    local_rows = jnp.dot(
        picks.astype(jnp.bfloat16), tokens, preferred_element_type=jnp.float32
    ).astype(jnp.bfloat16)
    local_cot = jnp.dot(weighted, cotangent.astype(jnp.float32), precision=highest).astype(
        jnp.bfloat16
    )
    w_g = w_gate[0]
    w_u = w_up[0]
    w_o = w_out[0]
    rows_blk = rows_in((local_rows,))[0]
    gate_share, up_share = reduce_acts((project_cols(rows_blk, w_g), project_cols(rows_blk, w_u)))
    active, hidden_share = swiglu(gate_share, up_share)
    hidden = collect((hidden_share,))[0]
    term_out = jnp.dot(hidden, w_o, preferred_element_type=jnp.float32)
    back_out = results_back((term_out,))[0]
    mixed = token_sums((combine(weighted, back_out),))[0]
    cot_blk = rows_in((local_cot,))[0]
    dh_share = reduce_acts((project_cols(cot_blk, w_o),))[0]
    gg_share, gu_share = swiglu_grad(gate_share, up_share, active, dh_share)
    grad_gate, grad_up = collect((gg_share, gu_share))
    term_grad = jnp.dot(grad_gate, w_g, preferred_element_type=jnp.float32) + jnp.dot(
        grad_up, w_u, preferred_element_type=jnp.float32
    )
    back_grad = results_back((term_grad,))[0]
    d_tokens = token_sums((combine(picks, back_grad),))[0]
    d_out = project_rows(hidden, cot_blk).astype(jnp.bfloat16)
    d_gate = project_rows(grad_gate, rows_blk).astype(jnp.bfloat16)
    d_up = project_rows(grad_up, rows_blk).astype(jnp.bfloat16)
    return (
        mixed.astype(jnp.bfloat16),
        d_tokens.astype(jnp.bfloat16),
        d_gate[None],
        d_up[None],
        d_out[None],
    )


def solution(mesh):
    return jax.shard_map(
        per_device,
        mesh=mesh,
        in_specs=(
            P("dp", None),
            P("dp", None),
            P("dp", None),
            P("expert", "tensor", "dp"),
            P("expert", "tensor", "dp"),
            P("expert", "tensor", "dp"),
            P("dp", None),
        ),
        out_specs=(
            P("dp", ("expert", "tensor")),
            P("dp", ("expert", "tensor")),
            P("expert", "tensor", "dp"),
            P("expert", "tensor", "dp"),
            P("expert", "tensor", "dp"),
        ),
        check_vma=False,
    )
```

profile of v0, /device:TPU:32, one launch (start us, length us, event | category | flops | bytes accessed | tf_op | source)
XLA Modules:
  0.0 911.0 jit_solution(1056512536293596920)
XLA Ops:
  7.2 0.8 copy.36
  8.0 0.1 copy.38
  8.1 0.1 reshape.95
  8.2 0.2 reduce-window_clone.1
  8.4 0.5 broadcast.56
  8.9 0.7 reduce.3
  9.6 0.1 reshape.94
  9.7 0.1 copy.37
  9.7 0.7 convert_reduce_fusion
  10.5 1.0 convolution_convert_fusion.1
  11.5 0.1 all_to_all.54
  11.6 0.1 copy.54
  11.7 0.8 reshape.120
  12.5 28.6 %all-to-all-start = ((bf16[32,2,480]{2,1,0:T(2,128)(2,1)}), bf16[32,2,480]{2,1,0:T(2,128)(2,1)S(1)}, u32[]{:S(2)}, u32[]{:S(2)}) async-start(bf16[32,2,480]{2,1,0:T(2,128)(2,1)} %reshape.120), calls=%async_computation | async-start | bytes 131072 | tf_op jit(solution)/shard_map/all_to_all | solution.py:28
  41.1 1.1 convolution_convert_fusion
  42.2 0.1 all_to_all.61
  42.4 0.8 reshape.124
  43.2 22.6 %all-to-all-done = bf16[32,2,480]{2,1,0:T(2,128)(2,1)S(1)} async-done(((bf16[32,2,480]{2,1,0:T(2,128)(2,1)}), bf16[32,2,480]{2,1,0:T(2,128)(2,1)S(1)}, u32[]{:S(2)}, u32[]{:S(2)}) %all-to-all-start) | async-done | bytes 61472 | tf_op jit(solution)/shard_map/all_to_all | solution.py:28
  65.8 4.8 all-to-all-start.2
  70.7 0.1 reshape.121
  70.8 0.1 all_to_all.57
  70.9 2.1 fusion.8
  73.0 1.1 fusion.12
  74.1 20.0 %all-to-all-done.2 = bf16[32,2,480]{2,1,0:T(2,128)(2,1)S(1)} async-done(((bf16[32,2,480]{2,1,0:T(2,128)(2,1)}), bf16[32,2,480]{2,1,0:T(2,128)(2,1)S(1)}, u32[]{:S(2)}, u32[]{:S(2)}) %all-to-all-start.2) | async-done | bytes 61472 | tf_op jit(solution)/shard_map/all_to_all | solution.py:28
  94.1 0.1 reshape.125
  94.2 0.1 all_to_all.64
  94.3 1.1 fusion.5
  95.4 1.3 dynamic-slice
  97.4 250.0 %all-reduce.6.cloned.1.call-done = (f32[160,1024]{1,0:T(8,128)}, f32[160,1024]{1,0:T(8,128)}, f32[160,1024]{1,0:T(8,128)}) async-done(((f32[160,1024]{1,0:T(8,128)}, f32[160,1024]{1,0:T(8,128)}, f32[160,1024]{1,0:T(8,128)}), (f32[160,1024]{1,0:T(8,128)}, f32[160,1024]{1,0:T(8,128)}, f32[160,1024]{1,0:T(8,128)})) %all-reduce.6.cloned.1.call-update) | async-done | bytes 1966096
  347.4 1.0 fusion.17
  348.4 56.2 %all-gather = bf16[32,5,1024]{2,1,0:T(8,128)(2,1)S(1)} all-gather(bf16[1,5,1024]{2,1,0:T(8,128)(2,1)S(1)} %get-tuple-element.14), channel_id=1, replica_groups=mesh['dp'=32,'expert'=4,'tensor'=8] {'dp'}, dimensions={0}, use_global_device_ids=true | all-gather | bytes 337920 | tf_op jit(solution)/shard_map/all_gather | solution.py:38
  404.6 0.4 fusion.3
  405.0 0.1 copy.41
  405.1 0.9 reshape.122
  405.9 15.2 %all-to-all-start.1 = ((f32[32,1,960]{2,1,0:T(1,128)}), f32[32,1,960]{2,1,0:T(1,128)S(1)}, u32[]{:S(2)}, u32[]{:S(2)}) async-start(f32[32,1,960]{2,1,0:T(1,128)} %reshape.122), calls=%async_computation.1 | async-start | bytes 262144 | tf_op jit(solution)/shard_map/all_to_all | solution.py:44
  421.2 60.1 %all-gather.1 = bf16[32,5,1024]{2,1,0:T(8,128)(2,1)S(1)} all-gather(bf16[1,5,1024]{2,1,0:T(8,128)(2,1)S(1)} %get-tuple-element.13), channel_id=1, replica_groups=mesh['dp'=32,'expert'=4,'tensor'=8] {'dp'}, dimensions={0}, use_global_device_ids=true | all-gather | bytes 337920 | tf_op jit(solution)/shard_map/all_gather | solution.py:38
  481.3 0.1 reshape.99
  481.4 59.2 %all-gather.2 = bf16[32,5,1024]{2,1,0:T(8,128)(2,1)S(1)} all-gather(bf16[1,5,1024]{2,1,0:T(8,128)(2,1)S(1)} %get-tuple-element.12), channel_id=1, replica_groups=mesh['dp'=32,'expert'=4,'tensor'=8] {'dp'}, dimensions={0}, use_global_device_ids=true | all-gather | bytes 337920 | tf_op jit(solution)/shard_map/all_gather | solution.py:38
  540.7 0.1 reshape.101
  540.8 0.3 fusion.10
  541.1 0.3 convolution_add_fusion
  541.4 0.9 reshape.126
  542.3 19.1 %all-to-all-start.3 = ((f32[32,1,960]{2,1,0:T(1,128)}), f32[32,1,960]{2,1,0:T(1,128)S(1)}, u32[]{:S(2)}, u32[]{:S(2)}) async-start(f32[32,1,960]{2,1,0:T(1,128)} %reshape.126), calls=%async_computation.3 | async-start | bytes 262144 | tf_op jit(solution)/shard_map/all_to_all | solution.py:44
  561.4 0.5 broadcast.57
  561.9 0.9 reduce.4
  562.9 0.1 reshape.123
  563.0 0.1 copy.42
  563.1 0.1 all_to_all.60
  563.2 6.7 convolution_bitcast_fusion.1
  569.9 0.2 reduce-scatter.9.cloned.1.call-start
  570.2 0.1 reshape.97
  570.3 17.2 %all-to-all-done.3 = f32[32,1,960]{2,1,0:T(1,128)S(1)} async-done(((f32[32,1,960]{2,1,0:T(1,128)}), f32[32,1,960]{2,1,0:T(1,128)S(1)}, u32[]{:S(2)}, u32[]{:S(2)}) %all-to-all-start.3) | async-done | bytes 122912 | tf_op jit(solution)/shard_map/all_to_all | solution.py:44
  587.5 1.0 reduce.5
  588.5 0.1 reshape.127
  588.6 0.1 copy.44
  588.7 0.1 all_to_all.68
  588.8 6.8 convolution_bitcast_fusion
  595.6 1.1 fusion
  596.6 1.1 fusion.1
  597.7 1.1 fusion.2
  598.7 138.4 %reduce-scatter.7.cloned.1.call-done = f32[192,8]{1,0:T(8,128)} async-done(((f32[6144,8]{1,0:T(8,128)}), f32[192,8]{1,0:T(8,128)}) %reduce-scatter.7.cloned.1.call-update) | async-done | bytes 6160
  737.2 1.6 copy.46
  738.7 164.2 %reduce-scatter.9.cloned.1.call-done = f32[192,8]{1,0:T(8,128)} async-done(((f32[6144,8]{1,0:T(8,128)}), f32[192,8]{1,0:T(8,128)}) %reduce-scatter.9.cloned.1.call-update) | async-done | bytes 6160
  902.9 1.6 copy.48
  (18 shorter events, 0.3 us)
Async XLA Ops:
  7.2 87.1 %copy-start = (bf16[1,1024,192]{1,2,0:T(8,128)(2,1)S(1)}, bf16[1,1024,192]{1,2,0:T(8,128)(2,1)}, u32[]{:S(2)}) copy-start(bf16[1,1024,192]{1,2,0:T(8,128)(2,1)} %param.12) | copy-start | bytes 1179652
  7.2 65.8 %copy-start.1 = (bf16[1,1024,192]{1,2,0:T(8,128)(2,1)S(1)}, bf16[1,1024,192]{1,2,0:T(8,128)(2,1)}, u32[]{:S(2)}) copy-start(bf16[1,1024,192]{1,2,0:T(8,128)(2,1)} %param.10) | copy-start | bytes 1179652
  12.5 53.3 %all-to-all-start = ((bf16[32,2,480]{2,1,0:T(2,128)(2,1)}), bf16[32,2,480]{2,1,0:T(2,128)(2,1)S(1)}, u32[]{:S(2)}, u32[]{:S(2)}) async-start(bf16[32,2,480]{2,1,0:T(2,128)(2,1)} %reshape.120), calls=%async_computation | async-start | bytes 131072 | tf_op jit(solution)/shard_map/all_to_all | solution.py:28
  65.8 28.2 %all-to-all-start.2 = ((bf16[32,2,480]{2,1,0:T(2,128)(2,1)}), bf16[32,2,480]{2,1,0:T(2,128)(2,1)S(1)}, u32[]{:S(2)}, u32[]{:S(2)}) async-start(bf16[32,2,480]{2,1,0:T(2,128)(2,1)} %reshape.124), calls=%async_computation.2 | async-start | bytes 131072 | tf_op jit(solution)/shard_map/all_to_all | solution.py:28
  70.6 276.8 %all-reduce.6.cloned.1.call-start = ((), (), s32[]{:S(2)}) async-start(), calls=%async_computation.8 | async-start | bytes 3932160
  347.4 193.7 %copy-start.2 = (bf16[1,1024,192]{1,2,0:T(8,128)(2,1)S(1)}, bf16[1,1024,192]{1,2,0:T(8,128)(2,1)}, u32[]{:S(2)}) copy-start(bf16[1,1024,192]{1,2,0:T(8,128)(2,1)} %param.11) | copy-start | bytes 1179652
  405.9 136.4 %all-to-all-start.1 = ((f32[32,1,960]{2,1,0:T(1,128)}), f32[32,1,960]{2,1,0:T(1,128)S(1)}, u32[]{:S(2)}, u32[]{:S(2)}) async-start(f32[32,1,960]{2,1,0:T(1,128)} %reshape.122), calls=%async_computation.1 | async-start | bytes 262144 | tf_op jit(solution)/shard_map/all_to_all | solution.py:44
  542.3 45.2 %all-to-all-start.3 = ((f32[32,1,960]{2,1,0:T(1,128)}), f32[32,1,960]{2,1,0:T(1,128)S(1)}, u32[]{:S(2)}, u32[]{:S(2)}) async-start(f32[32,1,960]{2,1,0:T(1,128)} %reshape.126), calls=%async_computation.3 | async-start | bytes 262144 | tf_op jit(solution)/shard_map/all_to_all | solution.py:44
  561.4 175.8 %reduce-scatter.7.cloned.1.call-start = ((), (), s32[]{:S(2)}) async-start(), calls=%async_computation.6 | async-start | bytes 3244032
  569.9 333.0 %reduce-scatter.9.cloned.1.call-start = ((), (), s32[]{:S(2)}) async-start(), calls=%async_computation.7 | async-start | bytes 3244032
Sparse Core Ops, SparseCore 0:
  95.5 251.7 all-reduce.5
  570.1 167.0 reduce-scatter.6
  740.6 162.3 reduce-scatter.8
where the time goes:
time: 912 us; the launch traced here: 911 us
  waiting for transfers between devices  613 us (67%)
  blocking collectives  176 us (19%)
  starting transfers between devices  68 us (7%)
  matrix products  24 us (3%)
  between operations  14.6 us (2%)
  local copies, waits for them, and re-layouts  11.8 us (1%)
    unnamed x6, waiting for transfers between devices  553 us
    all_gather x3, blocking collectives, collect(): lax.all_gather(shortened(parts), 'dp', axis=0, tiled=True)  176 us
    all_to_all x2, waiting for transfers between devices, rows_in(): lax.all_to_all(parts[0], 'dp', split_axis=1, concat_axis=0, tiled=True)  42.6 us
    all_to_all x2, starting transfers between devices, results_back(): lax.all_to_all(parts[0], 'dp', split_axis=0, concat_axis=1, tiled=True)  34.3 us
    all_to_all x2, starting transfers between devices, rows_in(): lax.all_to_all(parts[0], 'dp', split_axis=1, concat_axis=0, tiled=True)  33.4 us
  transfers between devices with their start and end apart: 7, of which 6 were waited for; matrix products, arithmetic and copies ran while one was open for 3% of the time, Pallas kernels for 0%

commit v1 on v0

v1 whole, which is shorter than its diff:
```python
import functools

import jax
import jax.numpy as jnp
from jax import lax
from jax.experimental import pallas as pl
from jax.experimental.pallas import tpu as pltpu
from jax.sharding import PartitionSpec as P

MESH = pl.DeviceIdType.MESH
F32 = jnp.float32
BF16 = jnp.bfloat16
LANES = 128
EMPTY = -1024.0


def iota(shape, axis):
    return lax.broadcasted_iota(jnp.int32, shape, axis)


def nn(a, b):
    return jnp.dot(a, b, preferred_element_type=F32)


def nt(a, b):
    return lax.dot_general(a, b, (((1,), (1,)), ((), ())), preferred_element_type=F32)


def tn(a, b):
    return lax.dot_general(a, b, (((0,), (0,)), ((), ())), preferred_element_type=F32)


def split3(v):
    hi = v.astype(BF16).astype(F32)
    mid = (v - hi).astype(BF16).astype(F32)
    return hi, mid, v - hi - mid


def source_block(index, feats, tok_ref, cot_ref, ids_ref, gates_ref):
    group = tok_ref.shape[0]
    wide = 2 * feats

    def features(ref):
        start = pl.multiple_of((index // 2) * wide, LANES)
        pair = ref[:, pl.ds(start, wide)].astype(F32)
        turned = pltpu.roll(pair, feats, 1)
        odd = lax.rem(jnp.full((group, wide), index, jnp.int32), 2) == 1
        return jnp.where(odd, turned, pair)[:, :256]

    eye = iota((group, group), 0) == iota((group, group), 1)
    before = iota((group, group), 1) < iota((group, group), 0)

    def column(row):
        spread = jnp.broadcast_to(row, (group, group))
        return jnp.sum(jnp.where(eye, spread, 0.0), axis=1, keepdims=True)

    ids = ids_ref[...].astype(F32)
    id_rows = [ids[k : k + 1, :] for k in range(2)]
    id_cols = [column(row) for row in id_rows]
    gate_cols = [column(gates_ref[k : k + 1, :]) for k in range(2)]

    def slots(k):
        own = jnp.broadcast_to(id_cols[k], (group, group))
        same = [
            (own == jnp.broadcast_to(row, (group, group))).astype(F32) for row in id_rows
        ]
        return jnp.sum(jnp.where(before, same[0] + same[1], 0.0), axis=1, keepdims=True)

    lane = iota((group, 256), 1)

    def per_expert(offset, values, other):
        at = (lane - offset).astype(F32)
        return jnp.where(
            at == id_cols[0], values[0], jnp.where(at == id_cols[1], values[1], other)
        )

    parts = [split3(column) for column in gate_cols]
    meta = per_expert(feats, [slots(0), slots(1)], EMPTY)
    for n in range(3):
        gate = per_expert(feats + 8 * (n + 1), [parts[0][n], parts[1][n]], 0.0)
        meta = jnp.where(lane >= feats + 8 * (n + 1), gate, meta)

    def joined(ref):
        return jnp.where(lane < feats, features(ref), meta)

    return jnp.concatenate([joined(tok_ref), joined(cot_ref)], axis=0).astype(BF16)


def kernel(
    sizes,
    tok_ref, ids_ref, gates_ref, wg_ref, wu_ref, wo_ref, cot_ref,
    mixed_ref, dtok_ref, dg_ref, du_ref, do_ref,
    blk, gathered, select, gate_mat, rows_buf, part, from_left, from_right,
    acts, wide_acts, terms, outgo, income, last, final,
    swap_sem, plane_send, plane_recv, right_send, right_recv, left_send, left_recv,
    ag_right_send, ag_right_recv, ag_left_send, ag_left_recv,
    back_send, back_recv, end_sem,
):
    n, tensor, capacity = sizes
    feats, hidden_units = wg_ref.shape
    group = tok_ref.shape[0]
    rows_n = capacity * n
    hops_right = n // 2
    hops_left = n - 1 - hops_right
    lane_blocks = hidden_units // LANES
    chunk = part.shape[2]

    z = lax.axis_index("dp")
    e = lax.axis_index("expert")
    t = lax.axis_index("tensor")
    index = e * tensor + t
    right = (lax.rem(z + 1, n), e, t)
    left = (lax.rem(z + n - 1, n), e, t)
    partner = (index, z // tensor, lax.rem(z, tensor))
    away = z != index

    def peer(j):
        return (z, j // tensor, lax.rem(j, tensor))

    barrier = pltpu.get_barrier_semaphore()

    def greet(k, _):
        j = lax.rem(index + k, n)
        pl.semaphore_signal(barrier, inc=1, device_id=peer(j), device_id_type=MESH)
        return 0

    lax.fori_loop(1, n, greet, 0)
    for neighbour in (left, right):
        pl.semaphore_signal(barrier, inc=1, device_id=neighbour, device_id_type=MESH)

    @pl.when(away)
    def _():
        pl.semaphore_signal(barrier, inc=1, device_id=partner, device_id_type=MESH)

    blk[...] = source_block(index, feats, tok_ref, cot_ref, ids_ref, gates_ref)
    pl.semaphore_wait(barrier, n + 1 + jnp.where(away, 1, 0))

    def swap():
        return pltpu.make_async_remote_copy(
            src_ref=blk, dst_ref=gathered.at[z], send_sem=swap_sem.at[0],
            recv_sem=swap_sem.at[1], device_id=partner, device_id_type=MESH,
        )

    @pl.when(away)
    def _():
        swap().start()
        swap().wait()

    @pl.when(jnp.logical_not(away))
    def _():
        gathered[index] = blk[...]

    def spread(k):
        j = lax.rem(index + k, n)
        return pltpu.make_async_remote_copy(
            src_ref=gathered.at[index], dst_ref=gathered.at[index],
            send_sem=plane_send.at[k], recv_sem=plane_recv.at[index],
            device_id=peer(j), device_id_type=MESH,
        )

    def arrival(k):
        j = lax.rem(index + n - k, n)
        return pltpu.make_async_remote_copy(
            src_ref=gathered.at[j], dst_ref=gathered.at[j],
            send_sem=plane_send.at[k], recv_sem=plane_recv.at[j],
            device_id=peer(j), device_id_type=MESH,
        )

    lax.fori_loop(1, n, lambda k, _: (spread(k).start(), 0)[1], 0)
    lax.fori_loop(1, n, lambda k, _: (arrival(k).wait_recv(), 0)[1], 0)

    lines = n * 2 * group
    block = gathered[...].reshape(lines, 256)
    meta = block[:, LANES:]
    base = feats - LANES
    pick = (iota((LANES, 2 * rows_n), 0) == base + e).astype(F32).astype(BF16)
    slot = nn(meta, pick)
    line = iota((lines, 2 * rows_n), 0)
    inner = lax.rem(line, 2 * group)
    place = capacity * (line // (2 * group)) + jnp.where(inner < group, 0, rows_n)
    sel = (slot + place.astype(F32) == iota((lines, 2 * rows_n), 1).astype(F32)).astype(F32)
    sel = sel.astype(BF16)
    select[...] = sel
    depth = iota((LANES, feats), 0) - base - e
    gate_pick = ((depth == 8) | (depth == 16) | (depth == 24)).astype(F32).astype(BF16)
    gate = nn(meta, gate_pick)
    gate_mat[...] = gate
    is_token = lax.rem(iota((lines, feats), 0), 2 * group) < group
    scaled = (block[:, :feats].astype(F32) * jnp.where(is_token, 1.0, gate)).astype(BF16)
    rows_all = tn(sel, scaled).astype(BF16)
    rows_buf[...] = rows_all
    rows = rows_all[:rows_n]
    cot_rows = rows_all[rows_n:]

    for a, (left_arg, w_ref) in enumerate(
        ((rows, wg_ref), (rows, wu_ref), (cot_rows, wo_ref))
    ):
        product = nn(left_arg, w_ref[...])
        for r in range(rows_n // chunk):
            for c in range(lane_blocks):
                part[r * lane_blocks + c, a] = product[
                    r * chunk : (r + 1) * chunk, c * LANES : (c + 1) * LANES
                ]

    def to_right(s, a, src):
        return pltpu.make_async_remote_copy(
            src_ref=src, dst_ref=from_left.at[s, a], send_sem=right_send.at[s, a],
            recv_sem=right_recv.at[s, a], device_id=right, device_id_type=MESH,
        )

    def to_left(s, a, src):
        return pltpu.make_async_remote_copy(
            src_ref=src, dst_ref=from_right.at[s, a], send_sem=left_send.at[s, a],
            recv_sem=left_recv.at[s, a], device_id=left, device_id_type=MESH,
        )

    def right_chunk(s):
        return lax.rem(z + hops_right - s + n, n)

    def left_chunk(s):
        return lax.rem(z - hops_left + s + n, n)

    def right_step(s, a):
        held = from_left.at[s - 1, a]
        to_right(s - 1, a, held).wait_recv()
        held[...] += part[right_chunk(s), a]
        to_right(s, a, held).start()

    def left_step(s, a):
        held = from_right.at[s - 1, a]
        to_left(s - 1, a, held).wait_recv()
        held[...] += part[left_chunk(s), a]
        to_left(s, a, held).start()

    for a in range(3):
        to_right(0, a, part.at[right_chunk(0), a]).start()
        to_left(0, a, part.at[left_chunk(0), a]).start()

    def both(s, _):
        for a in range(3):
            right_step(s, a)
            left_step(s, a)
        return 0

    lax.fori_loop(1, hops_left, both, 0)
    for s in range(hops_left, hops_right):
        for a in range(3):
            right_step(s, a)
    sums = []
    for a in range(3):
        to_right(hops_right - 1, a, from_left.at[hops_right - 1, a]).wait_recv()
        to_left(hops_left - 1, a, from_right.at[hops_left - 1, a]).wait_recv()
        sums.append(
            from_left[hops_right - 1, a] + from_right[hops_left - 1, a] + part[z, a]
        )

    gate_act, up_act, d_hidden = sums
    sig = jax.nn.sigmoid(gate_act)
    active = gate_act * sig
    grad_gate = d_hidden * up_act * (sig * (1.0 + gate_act * (1.0 - sig)))
    grad_up = d_hidden * active
    pad = acts.shape[1] - 3 * chunk
    acts[z] = jnp.concatenate(
        [active * up_act, grad_gate, grad_up, jnp.zeros((pad, LANES), F32)], axis=0
    ).astype(BF16)

    def ag_right(s, owner):
        return pltpu.make_async_remote_copy(
            src_ref=acts.at[owner], dst_ref=acts.at[owner], send_sem=ag_right_send.at[s],
            recv_sem=ag_right_recv.at[s], device_id=right, device_id_type=MESH,
        )

    def ag_left(s, owner):
        return pltpu.make_async_remote_copy(
            src_ref=acts.at[owner], dst_ref=acts.at[owner], send_sem=ag_left_send.at[s],
            recv_sem=ag_left_recv.at[s], device_id=left, device_id_type=MESH,
        )

    def unpack(owner):
        piece = acts[owner].astype(F32)
        row = pl.multiple_of((owner // lane_blocks) * chunk, 8)
        col = pl.multiple_of(lax.rem(owner, lane_blocks) * LANES, LANES)
        for a in range(3):
            wide_acts[a, pl.ds(row, chunk), pl.ds(col, LANES)] = piece[
                a * chunk : (a + 1) * chunk
            ]

    def owner_right(s):
        return lax.rem(z - s + n, n)

    def owner_left(s):
        return lax.rem(z + s, n)

    ag_right(0, z).start()
    ag_left(0, z).start()
    unpack(z)

    def ag_both(s, _):
        ag_right(s - 1, owner_right(s)).wait_recv()
        ag_right(s, owner_right(s)).start()
        ag_left(s - 1, owner_left(s)).wait_recv()
        ag_left(s, owner_left(s)).start()
        unpack(owner_right(s))
        unpack(owner_left(s))
        return 0

    lax.fori_loop(1, hops_left, ag_both, 0)
    for s in range(hops_left, hops_right):
        ag_right(s - 1, owner_right(s)).wait_recv()
        ag_right(s, owner_right(s)).start()
        unpack(owner_right(s))
    ag_left(hops_left - 1, owner_left(hops_left)).wait_recv()
    unpack(owner_left(hops_left))
    ag_right(hops_right - 1, owner_right(hops_right)).wait_recv()
    unpack(owner_right(hops_right))

    hidden_all = wide_acts[0].astype(BF16)
    gg_all = wide_acts[1].astype(BF16)
    gu_all = wide_acts[2].astype(BF16)

    terms[:rows_n] = nt(hidden_all, wo_ref[...])
    terms[rows_n:] = nt(gg_all, wg_ref[...]) + nt(gu_all, wu_ref[...])
    whole = terms[...]
    high = whole.astype(BF16)
    low = (whole - high.astype(F32)).astype(BF16)
    table = select[...]
    per_token = nn(table, high) + nn(table, low)
    per_token = per_token * jnp.where(is_token, gate_mat[...], 1.0)
    outgo[...] = per_token.reshape(n, 2 * group, feats)

    def send_back(k):
        j = lax.rem(index + k, n)
        return pltpu.make_async_remote_copy(
            src_ref=outgo.at[j], dst_ref=income.at[index],
            send_sem=back_send.at[k], recv_sem=back_recv.at[index],
            device_id=peer(j), device_id_type=MESH,
        )

    def got_back(k):
        j = lax.rem(index + n - k, n)
        return pltpu.make_async_remote_copy(
            src_ref=outgo.at[j], dst_ref=income.at[j],
            send_sem=back_send.at[k], recv_sem=back_recv.at[j],
            device_id=peer(j), device_id_type=MESH,
        )

    lax.fori_loop(1, n, lambda k, _: (send_back(k).start(), 0)[1], 0)
    income[index] = outgo[index]

    rows_kept = rows_buf[:rows_n]
    do_ref[...] = tn(rows_buf[rows_n:], hidden_all).astype(BF16)
    dg_ref[...] = tn(rows_kept, gg_all).astype(BF16)
    du_ref[...] = tn(rows_kept, gu_all).astype(BF16)

    lax.fori_loop(1, n, lambda k, _: (got_back(k).wait_recv(), 0)[1], 0)
    last[...] = jnp.sum(income[...], axis=0).astype(BF16)

    def finish():
        return pltpu.make_async_remote_copy(
            src_ref=last, dst_ref=final, send_sem=end_sem.at[0],
            recv_sem=end_sem.at[1], device_id=partner, device_id_type=MESH,
        )

    @pl.when(away)
    def _():
        finish().start()

    @pl.when(jnp.logical_not(away))
    def _():
        final[...] = last[...]

    def sent_plane(k, _):
        spread(k).wait_send()
        send_back(k).wait_send()
        return 0

    lax.fori_loop(1, n, sent_plane, 0)

    def sent_right(s, _):
        for a in range(3):
            to_right(s, a, from_left.at[s, a]).wait_send()
        ag_right(s, z).wait_send()
        return 0

    lax.fori_loop(0, hops_right, sent_right, 0)

    def sent_left(s, _):
        for a in range(3):
            to_left(s, a, from_right.at[s, a]).wait_send()
        ag_left(s, z).wait_send()
        return 0

    lax.fori_loop(0, hops_left, sent_left, 0)

    @pl.when(away)
    def _():
        finish().wait()

    done = final[...].astype(F32)
    mixed_ref[...] = done[:group].astype(BF16)
    dtok_ref[...] = done[group:].astype(BF16)


def per_device(n, tensor, experts, tokens, expert_ids, gates, w_gate, w_up, w_out, cotangent):
    group, model = tokens.shape
    _, hidden_units, feats = w_gate.shape
    capacity = 2 * (group // experts) + 1
    rows_n = capacity * n
    chunk = rows_n * (hidden_units // LANES) // n
    hops_right = n // 2
    hops_left = n - 1 - hops_right
    packed = -(-3 * chunk // 16) * 16
    vmem = pl.BlockSpec(memory_space=pltpu.VMEM)
    dma = pltpu.SemaphoreType.DMA
    weight = jax.ShapeDtypeStruct((feats, hidden_units), BF16)
    small = jax.ShapeDtypeStruct((group, feats), BF16)
    mixed, d_tokens, d_gate, d_up, d_out = pl.pallas_call(
        functools.partial(kernel, (n, tensor, capacity)),
        out_shape=(small, small, weight, weight, weight),
        in_specs=[vmem] * 7,
        out_specs=(vmem,) * 5,
        scratch_shapes=[
            pltpu.VMEM((2 * group, 256), BF16),
            pltpu.VMEM((n, 2 * group, 256), BF16),
            pltpu.VMEM((n * 2 * group, 2 * rows_n), BF16),
            pltpu.VMEM((n * 2 * group, feats), F32),
            pltpu.VMEM((2 * rows_n, feats), BF16),
            pltpu.VMEM((n, 3, chunk, LANES), F32),
            pltpu.VMEM((hops_right, 3, chunk, LANES), F32),
            pltpu.VMEM((hops_left, 3, chunk, LANES), F32),
            pltpu.VMEM((n, packed, LANES), BF16),
            pltpu.VMEM((3, rows_n, hidden_units), F32),
            pltpu.VMEM((2 * rows_n, feats), F32),
            pltpu.VMEM((n, 2 * group, feats), F32),
            pltpu.VMEM((n, 2 * group, feats), F32),
            pltpu.VMEM((2 * group, feats), BF16),
            pltpu.VMEM((2 * group, feats), BF16),
            dma((2,)),
            dma((n,)),
            dma((n,)),
            dma((hops_right, 3)),
            dma((hops_right, 3)),
            dma((hops_left, 3)),
            dma((hops_left, 3)),
            dma((hops_right,)),
            dma((hops_right,)),
            dma((hops_left,)),
            dma((hops_left,)),
            dma((n,)),
            dma((n,)),
            dma((2,)),
        ],
        compiler_params=pltpu.CompilerParams(
            collective_id=0, has_side_effects=True, vmem_limit_bytes=40 * 1024 * 1024
        ),
    )(
        tokens, expert_ids.T, gates.T, w_gate[0].T, w_up[0].T, w_out[0].T, cotangent
    )
    return (mixed, d_tokens, d_gate.T[None], d_up.T[None], d_out.T[None])


def solution(mesh):
    sizes = (mesh.shape["dp"], mesh.shape["tensor"], mesh.shape["expert"])
    return jax.shard_map(
        functools.partial(per_device, *sizes),
        mesh=mesh,
        in_specs=(
            P("dp", None),
            P("dp", None),
            P("dp", None),
            P("expert", "tensor", "dp"),
            P("expert", "tensor", "dp"),
            P("expert", "tensor", "dp"),
            P("dp", None),
        ),
        out_specs=(
            P("dp", ("expert", "tensor")),
            P("dp", ("expert", "tensor")),
            P("expert", "tensor", "dp"),
            P("expert", "tensor", "dp"),
            P("expert", "tensor", "dp"),
        ),
        check_vma=False,
    )
```

time: 912 us -> 182 us (0.20)
  the two profiles are of different devices: /device:TPU:32 before, /device:TPU:6 now
where the time goes in v1:
time: 182 us
  Pallas kernels  172 us (95%)
  local copies, waits for them, and re-layouts  8.87 us (5%)
    pallas_call x1, Pallas kernels, per_device(): pl.pallas_call(functools.partial(kernel, (n, tensor, capacity)), out_shap...  172 us
    unnamed x19, local copies, waits for them, and re-layouts  8.87 us

profile of v1, /device:TPU:6, one launch (start us, length us, event | category | flops | bytes accessed | tf_op | source)
XLA Modules:
  0.0 181.9 jit_solution(5961179898956896976)
XLA Ops:
  0.6 0.0 copy-start.6
  0.6 0.0 copy-start.5
  0.7 0.7 copy-done.6
  1.3 0.0 copy-done.5
  1.3 0.0 copy-start
  1.3 1.0 copy-done
  2.3 0.0 copy-start.1
  2.3 1.0 copy-done.1
  3.3 0.0 copy-start.2
  3.3 1.0 copy-done.2
  4.3 0.0 copy-start.3
  4.3 0.9 copy-done.3
  5.2 0.0 copy-start.4
  5.2 0.9 copy-done.4
  6.1 172.4 %shard_map.110 = (bf16[8,192]{1,0:T(8,128)(2,1)S(1)}, bf16[8,192]{1,0:T(8,128)(2,1)S(1)}, bf16[192,1024]{1,0:T(8,128)(2,1)S(1)}, bf16[192,1024]{1,0:T(8,128)(2,1)S(1)}, bf16[192,1024]{1,0:T(8,128)(2,1)S(1)}) custom-call(bf16[8,6144]{1,0:T(8,128)(2,1)S(1)} %copy-done.3, s32[2,8]{1,0:T(2,128)S(1)} %bitcast.26, f32[2,8]{1,0:T(2,128)S(1)} %bitcast.27, ...), custom_call_target="tpu_custom_call" | custom-call | tf_op jit(solution)/shard_map/pallas_call | solution.py:417
  178.5 0.6 copy.17
  179.1 0.6 copy.18
  179.7 0.7 copy.19
  180.4 0.7 copy.20
  181.1 0.7 copy.21
Async XLA Ops:
  0.6 0.7 copy-start.6
  0.6 0.7 copy-start.5
  1.3 1.0 copy-start
  2.3 1.0 copy-start.1
  3.3 1.0 copy-start.2
  4.3 0.9 copy-start.3
  5.2 0.9 copy-start.4

commit v2 on v1

--- a/solution.py
+++ b/solution.py
@@ -12,6 +12,11 @@
 BF16 = jnp.bfloat16
 LANES = 128
 EMPTY = -1024.0
+STRIDE = 4
+PIECES = 2
+NEIGHBOURS = (1, -1, 2, -2, STRIDE, -STRIDE)
+HALF_RIGHT = 2
+HALF_LEFT = 1
 
 
 def iota(shape, axis):
@@ -88,29 +93,44 @@
 
 def kernel(
     sizes,
-    tok_ref, ids_ref, gates_ref, wg_ref, wu_ref, wo_ref, cot_ref,
+    tok_hbm, ids_hbm, gates_hbm, wg_hbm, wu_hbm, wo_hbm, cot_hbm,
     mixed_ref, dtok_ref, dg_ref, du_ref, do_ref,
-    blk, gathered, select, gate_mat, rows_buf, part, from_left, from_right,
+    tok_ref, ids_ref, gates_ref, wg_ref, wu_ref, wo_ref, cot_ref, load_sem,
+    blk, gathered, select, gate_mat, rows_buf, part, packed, near, half_out, half_in, full_out, full_in,
     acts, wide_acts, terms, outgo, income, last, final,
-    swap_sem, plane_send, plane_recv, right_send, right_recv, left_send, left_recv,
-    ag_right_send, ag_right_recv, ag_left_send, ag_left_recv,
-    back_send, back_recv, end_sem,
+    swap_sem, plane_send, plane_recv, near_send, near_recv, chain_send, chain_recv,
+    ag_send, ag_recv, share_send, share_recv, back_send, back_recv, end_sem,
 ):
     n, tensor, capacity = sizes
-    feats, hidden_units = wg_ref.shape
+    feats, hidden_units = wg_hbm.shape
     group = tok_ref.shape[0]
     rows_n = capacity * n
-    hops_right = n // 2
-    hops_left = n - 1 - hops_right
+    leaders = n // STRIDE
+    hops_right = leaders // 2
+    hops_left = leaders - 1 - hops_right
     lane_blocks = hidden_units // LANES
-    chunk = part.shape[2]
+    chunk = rows_n * lane_blocks // n
+    used, full = 3 * chunk, part.shape[1]
+    piece = full // PIECES
+
+    loads = [
+        pltpu.make_async_copy(src, dst, load_sem.at[k])
+        for k, (src, dst) in enumerate((
+            (tok_hbm, tok_ref), (cot_hbm, cot_ref), (ids_hbm, ids_ref), (gates_hbm, gates_ref),
+            (wg_hbm, wg_ref), (wu_hbm, wu_ref), (wo_hbm, wo_ref),
+        ))
+    ]
+    for load in loads:
+        load.start()
 
     z = lax.axis_index("dp")
     e = lax.axis_index("expert")
     t = lax.axis_index("tensor")
     index = e * tensor + t
-    right = (lax.rem(z + 1, n), e, t)
-    left = (lax.rem(z + n - 1, n), e, t)
+
+    def along(step):
+        return (lax.rem(z + step + n, n), e, t)
+
     partner = (index, z // tensor, lax.rem(z, tensor))
     away = z != index
 
@@ -118,6 +138,13 @@
         return (z, j // tensor, lax.rem(j, tensor))
 
     barrier = pltpu.get_barrier_semaphore()
+
+    @pl.when(away)
+    def _():
+        pl.semaphore_signal(barrier, inc=1, device_id=partner, device_id_type=MESH)
+
+    for step in NEIGHBOURS:
+        pl.semaphore_signal(barrier, inc=1, device_id=along(step), device_id_type=MESH)
 
     def greet(k, _):
         j = lax.rem(index + k, n)
@@ -125,15 +152,10 @@
         return 0
 
     lax.fori_loop(1, n, greet, 0)
-    for neighbour in (left, right):
-        pl.semaphore_signal(barrier, inc=1, device_id=neighbour, device_id_type=MESH)
-
-    @pl.when(away)
-    def _():
-        pl.semaphore_signal(barrier, inc=1, device_id=partner, device_id_type=MESH)
-
+    for load in loads[:4]:
+        load.wait()
     blk[...] = source_block(index, feats, tok_ref, cot_ref, ids_ref, gates_ref)
-    pl.semaphore_wait(barrier, n + 1 + jnp.where(away, 1, 0))
+    pl.semaphore_wait(barrier, n - 1 + len(NEIGHBOURS) + jnp.where(away, 1, 0))
 
     def swap():
         return pltpu.make_async_remote_copy(
@@ -192,127 +214,193 @@
     rows = rows_all[:rows_n]
     cot_rows = rows_all[rows_n:]
 
+    part[:, used:] = jnp.zeros((n, full - used, LANES), F32)
+    for load in loads[4:]:
+        load.wait()
     for a, (left_arg, w_ref) in enumerate(
         ((rows, wg_ref), (rows, wu_ref), (cot_rows, wo_ref))
     ):
         product = nn(left_arg, w_ref[...])
         for r in range(rows_n // chunk):
             for c in range(lane_blocks):
-                part[r * lane_blocks + c, a] = product[
+                part[r * lane_blocks + c, a * chunk : (a + 1) * chunk] = product[
                     r * chunk : (r + 1) * chunk, c * LANES : (c + 1) * LANES
                 ]
 
-    def to_right(s, a, src):
-        return pltpu.make_async_remote_copy(
-            src_ref=src, dst_ref=from_left.at[s, a], send_sem=right_send.at[s, a],
-            recv_sem=right_recv.at[s, a], device_id=right, device_id_type=MESH,
-        )
-
-    def to_left(s, a, src):
-        return pltpu.make_async_remote_copy(
-            src_ref=src, dst_ref=from_right.at[s, a], send_sem=left_send.at[s, a],
-            recv_sem=left_recv.at[s, a], device_id=left, device_id_type=MESH,
-        )
-
-    def right_chunk(s):
-        return lax.rem(z + hops_right - s + n, n)
-
-    def left_chunk(s):
-        return lax.rem(z - hops_left + s + n, n)
-
-    def right_step(s, a):
-        held = from_left.at[s - 1, a]
-        to_right(s - 1, a, held).wait_recv()
-        held[...] += part[right_chunk(s), a]
-        to_right(s, a, held).start()
-
-    def left_step(s, a):
-        held = from_right.at[s - 1, a]
-        to_left(s - 1, a, held).wait_recv()
-        held[...] += part[left_chunk(s), a]
-        to_left(s, a, held).start()
-
-    for a in range(3):
-        to_right(0, a, part.at[right_chunk(0), a]).start()
-        to_left(0, a, part.at[left_chunk(0), a]).start()
-
-    def both(s, _):
-        for a in range(3):
-            right_step(s, a)
-            left_step(s, a)
-        return 0
-
-    lax.fori_loop(1, hops_left, both, 0)
-    for s in range(hops_left, hops_right):
-        for a in range(3):
-            right_step(s, a)
-    sums = []
-    for a in range(3):
-        to_right(hops_right - 1, a, from_left.at[hops_right - 1, a]).wait_recv()
-        to_left(hops_left - 1, a, from_right.at[hops_left - 1, a]).wait_recv()
-        sums.append(
-            from_left[hops_right - 1, a] + from_right[hops_left - 1, a] + part[z, a]
-        )
+    def owner(step):
+        return lax.rem(z + step + n, n)
+
+    to_right = [STRIDE * (hops_right - s) for s in range(hops_right)]
+    to_left = [-STRIDE * (hops_left - s) for s in range(hops_left)]
+    order = []
+    for s in range(hops_right):
+        order += to_right[s : s + 1] + to_left[s : s + 1]
+    order += [0]
+    near_owners = {
+        1: order,
+        -1: order,
+        2: [v - STRIDE for v in to_right],
+        -2: to_left + [0],
+    }
+    near_base = {}
+    total = 0
+    for step, owners in near_owners.items():
+        near_base[step] = total
+        total += len(owners)
+
+    def near_copy(step, k):
+        at = near_base[step] + k
+        return pltpu.make_async_remote_copy(
+            src_ref=packed.at[at], dst_ref=near.at[at], send_sem=near_send.at[at],
+            recv_sem=near_recv.at[at], device_id=along(step), device_id_type=MESH,
+        )
+
+    def send_near(targets):
+        for target in targets:
+            for step, owners in near_owners.items():
+                if target in owners:
+                    k = owners.index(target)
+                    packed[near_base[step] + k] = part[owner(step + target)].astype(BF16)
+                    near_copy(step, k).start()
+
+    def targets_of(s):
+        return to_right[s : s + 1] + to_left[s : s + 1] if s < hops_right else [0]
+
+    def is_wide(way, s):
+        return s >= (HALF_RIGHT if way > 0 else HALF_LEFT)
+
+    def chain_copy(way, s, p):
+        number = s if way > 0 else hops_right + s
+        wide = is_wide(way, s)
+        out, into = (full_out, full_in) if wide else (half_out, half_in)
+        rows = pl.ds(p * piece, min(used, (p + 1) * piece) - p * piece if wide else piece)
+        return pltpu.make_async_remote_copy(
+            src_ref=out.at[number, rows], dst_ref=into.at[number, rows],
+            send_sem=chain_send.at[number, p], recv_sem=chain_recv.at[number, p],
+            device_id=along(way * STRIDE), device_id_type=MESH,
+        )
+
+    def arrived(way, s, p):
+        number = s if way > 0 else hops_right + s
+        chain_copy(way, s, p).wait_recv()
+        return (full_in if is_wide(way, s) else half_in)[
+            number, p * piece : (p + 1) * piece
+        ].astype(F32)
+
+    def around(target):
+        value = part[owner(target)]
+        for step, owners in near_owners.items():
+            if target in owners:
+                k = owners.index(target)
+                near_copy(step, k).wait_recv()
+                value = value + near[near_base[step] + k].astype(F32)
+        return value
+
+    def ways(s):
+        return ((1, to_right), (-1, to_left)) if s < hops_left else ((1, to_right),)
+
+    if used < full:
+        full_in[:, used:] = jnp.zeros((leaders - 1, full - used, LANES), F32)
+    send_near(targets_of(0))
+    send_near(targets_of(1))
+    for s in range(hops_right):
+        here = {way: around(targets[s]) for way, targets in ways(s)}
+        for p in range(PIECES):
+            for way, _ in ways(s):
+                value = here[way][p * piece : (p + 1) * piece]
+                if s > 0:
+                    value = value + arrived(way, s - 1, p)
+                number = s if way > 0 else hops_right + s
+                if is_wide(way, s):
+                    full_out[number, p * piece : (p + 1) * piece] = value
+                else:
+                    half_out[number, p * piece : (p + 1) * piece] = value.astype(BF16)
+                chain_copy(way, s, p).start()
+        if s + 2 <= hops_right:
+            send_near(targets_of(s + 2))
+        if s == hops_left and hops_left:
+            from_far_side = [arrived(-1, s - 1, p) for p in range(PIECES)]
+    value = around(0)
+    if hops_left:
+        value = value + jnp.concatenate(from_far_side, axis=0)
+    value = value + jnp.concatenate(
+        [arrived(1, hops_right - 1, p) for p in range(PIECES)], axis=0
+    )
+    sums = [value[a * chunk : (a + 1) * chunk] for a in range(3)]
 
     gate_act, up_act, d_hidden = sums
     sig = jax.nn.sigmoid(gate_act)
     active = gate_act * sig
     grad_gate = d_hidden * up_act * (sig * (1.0 + gate_act * (1.0 - sig)))
     grad_up = d_hidden * active
-    pad = acts.shape[1] - 3 * chunk
-    acts[z] = jnp.concatenate(
-        [active * up_act, grad_gate, grad_up, jnp.zeros((pad, LANES), F32)], axis=0
-    ).astype(BF16)
-
-    def ag_right(s, owner):
-        return pltpu.make_async_remote_copy(
-            src_ref=acts.at[owner], dst_ref=acts.at[owner], send_sem=ag_right_send.at[s],
-            recv_sem=ag_right_recv.at[s], device_id=right, device_id_type=MESH,
-        )
-
-    def ag_left(s, owner):
-        return pltpu.make_async_remote_copy(
-            src_ref=acts.at[owner], dst_ref=acts.at[owner], send_sem=ag_left_send.at[s],
-            recv_sem=ag_left_recv.at[s], device_id=left, device_id_type=MESH,
-        )
-
-    def unpack(owner):
-        piece = acts[owner].astype(F32)
-        row = pl.multiple_of((owner // lane_blocks) * chunk, 8)
-        col = pl.multiple_of(lax.rem(owner, lane_blocks) * LANES, LANES)
+    blank = [jnp.zeros((full - used, LANES), F32)] if used < full else []
+    acts[z] = jnp.concatenate([active * up_act, grad_gate, grad_up] + blank, axis=0).astype(BF16)
+
+    share_owners = {
+        1: order,
+        -1: order,
+        2: [-STRIDE * k for k in range(hops_right)],
+        -2: [STRIDE * k for k in range(hops_left + 1)],
+    }
+
+    def chain_back(way, s, held, p):
+        number = s if way > 0 else hops_right + s
+        place = acts.at[owner(held), pl.ds(p * piece, piece)]
+        return pltpu.make_async_remote_copy(
+            src_ref=place, dst_ref=place, send_sem=ag_send.at[number, p],
+            recv_sem=ag_recv.at[number, p], device_id=along(way * STRIDE), device_id_type=MESH,
+        )
+
+    def share(step, held, k):
+        at = near_base[step] + k
+        place = acts.at[owner(held)]
+        return pltpu.make_async_remote_copy(
+            src_ref=place, dst_ref=place, send_sem=share_send.at[at],
+            recv_sem=share_recv.at[at], device_id=along(step), device_id_type=MESH,
+        )
+
+    def unpack(held):
+        place = owner(held)
+        block = acts[place].astype(F32)
+        row = pl.multiple_of((place // lane_blocks) * chunk, 8)
+        col = pl.multiple_of(lax.rem(place, lane_blocks) * LANES, LANES)
         for a in range(3):
-            wide_acts[a, pl.ds(row, chunk), pl.ds(col, LANES)] = piece[
+            wide_acts[a, pl.ds(row, chunk), pl.ds(col, LANES)] = block[
                 a * chunk : (a + 1) * chunk
             ]
 
-    def owner_right(s):
-        return lax.rem(z - s + n, n)
-
-    def owner_left(s):
-        return lax.rem(z + s, n)
-
-    ag_right(0, z).start()
-    ag_left(0, z).start()
-    unpack(z)
-
-    def ag_both(s, _):
-        ag_right(s - 1, owner_right(s)).wait_recv()
-        ag_right(s, owner_right(s)).start()
-        ag_left(s - 1, owner_left(s)).wait_recv()
-        ag_left(s, owner_left(s)).start()
-        unpack(owner_right(s))
-        unpack(owner_left(s))
-        return 0
-
-    lax.fori_loop(1, hops_left, ag_both, 0)
-    for s in range(hops_left, hops_right):
-        ag_right(s - 1, owner_right(s)).wait_recv()
-        ag_right(s, owner_right(s)).start()
-        unpack(owner_right(s))
-    ag_left(hops_left - 1, owner_left(hops_left)).wait_recv()
-    unpack(owner_left(hops_left))
-    ag_right(hops_right - 1, owner_right(hops_right)).wait_recv()
-    unpack(owner_right(hops_right))
+    def pass_on(held):
+        for step, owners in share_owners.items():
+            if held in owners:
+                share(step, held, owners.index(held)).start()
+
+    def taken(distance):
+        for step, owners in share_owners.items():
+            for k, held in enumerate(owners):
+                if abs(held) == distance * STRIDE:
+                    share(step, held - step, k).wait_recv()
+                    unpack(held - step)
+
+    for p in range(PIECES):
+        for way, _ in ways(0):
+            chain_back(way, 0, 0, p).start()
+    pass_on(0)
+    unpack(0)
+    for s in range(1, hops_right + 1):
+        coming = [(1, -STRIDE * s if s < hops_right else STRIDE * s)]
+        if s <= hops_left:
+            coming.append((-1, STRIDE * s))
+        for p in range(PIECES):
+            for way, held in coming:
+                chain_back(way, s - 1, held, p).wait_recv()
+                if s < (hops_right if way > 0 else hops_left):
+                    chain_back(way, s, held, p).start()
+        for _, held in coming:
+            pass_on(held)
+        for _, held in coming:
+            unpack(held)
+        taken(s - 1)
+    taken(hops_right)
 
     hidden_all = wide_acts[0].astype(BF16)
     gg_all = wide_acts[1].astype(BF16)
@@ -376,21 +464,15 @@
 
     lax.fori_loop(1, n, sent_plane, 0)
 
-    def sent_right(s, _):
-        for a in range(3):
-            to_right(s, a, from_left.at[s, a]).wait_send()
-        ag_right(s, z).wait_send()
-        return 0
-
-    lax.fori_loop(0, hops_right, sent_right, 0)
-
-    def sent_left(s, _):
-        for a in range(3):
-            to_left(s, a, from_right.at[s, a]).wait_send()
-        ag_left(s, z).wait_send()
-        return 0
-
-    lax.fori_loop(0, hops_left, sent_left, 0)
+    for step, owners in near_owners.items():
+        for k in range(len(owners)):
+            near_copy(step, k).wait_send()
+            share(step, 0, k).wait_send()
+    for way, hops in ((1, hops_right), (-1, hops_left)):
+        for s in range(hops):
+            for p in range(PIECES):
+                chain_copy(way, s, p).wait_send()
+                chain_back(way, s, 0, p).wait_send()
 
     @pl.when(away)
     def _():
@@ -407,9 +489,11 @@
     capacity = 2 * (group // experts) + 1
     rows_n = capacity * n
     chunk = rows_n * (hidden_units // LANES) // n
-    hops_right = n // 2
-    hops_left = n - 1 - hops_right
-    packed = -(-3 * chunk // 16) * 16
+    leaders = n // STRIDE
+    hops = leaders - 1
+    nears = 3 * leaders
+    packed = -(-3 * chunk // (16 * PIECES)) * 16 * PIECES
+    hbm = pl.BlockSpec(memory_space=pltpu.HBM)
     vmem = pl.BlockSpec(memory_space=pltpu.VMEM)
     dma = pltpu.SemaphoreType.DMA
     weight = jax.ShapeDtypeStruct((feats, hidden_units), BF16)
@@ -417,17 +501,29 @@
     mixed, d_tokens, d_gate, d_up, d_out = pl.pallas_call(
         functools.partial(kernel, (n, tensor, capacity)),
         out_shape=(small, small, weight, weight, weight),
-        in_specs=[vmem] * 7,
+        in_specs=[hbm] * 7,
         out_specs=(vmem,) * 5,
         scratch_shapes=[
+            pltpu.VMEM(tokens.shape, BF16),
+            pltpu.VMEM((2, group), jnp.int32),
+            pltpu.VMEM((2, group), F32),
+            pltpu.VMEM((feats, hidden_units), BF16),
+            pltpu.VMEM((feats, hidden_units), BF16),
+            pltpu.VMEM((feats, hidden_units), BF16),
+            pltpu.VMEM(tokens.shape, BF16),
+            dma((7,)),
             pltpu.VMEM((2 * group, 256), BF16),
             pltpu.VMEM((n, 2 * group, 256), BF16),
             pltpu.VMEM((n * 2 * group, 2 * rows_n), BF16),
             pltpu.VMEM((n * 2 * group, feats), F32),
             pltpu.VMEM((2 * rows_n, feats), BF16),
-            pltpu.VMEM((n, 3, chunk, LANES), F32),
-            pltpu.VMEM((hops_right, 3, chunk, LANES), F32),
-            pltpu.VMEM((hops_left, 3, chunk, LANES), F32),
+            pltpu.VMEM((n, packed, LANES), F32),
+            pltpu.VMEM((nears, packed, LANES), BF16),
+            pltpu.VMEM((nears, packed, LANES), BF16),
+            pltpu.VMEM((hops, packed, LANES), BF16),
+            pltpu.VMEM((hops, packed, LANES), BF16),
+            pltpu.VMEM((hops, packed, LANES), F32),
+            pltpu.VMEM((hops, packed, LANES), F32),
             pltpu.VMEM((n, packed, LANES), BF16),
             pltpu.VMEM((3, rows_n, hidden_units), F32),
             pltpu.VMEM((2 * rows_n, feats), F32),
@@ -438,14 +534,14 @@
             dma((2,)),
             dma((n,)),
             dma((n,)),
-            dma((hops_right, 3)),
-            dma((hops_right, 3)),
-            dma((hops_left, 3)),
-            dma((hops_left, 3)),
-            dma((hops_right,)),
-            dma((hops_right,)),
-            dma((hops_left,)),
-            dma((hops_left,)),
+            dma((nears,)),
+            dma((nears,)),
+            dma((hops, PIECES)),
+            dma((hops, PIECES)),
+            dma((hops, PIECES)),
+            dma((hops, PIECES)),
+            dma((nears,)),
+            dma((nears,)),
             dma((n,)),
             dma((n,)),
             dma((2,)),

time: 182 us -> 141 us (0.77)
  the two profiles are of different devices: /device:TPU:6 before, /device:TPU:2 now
where the time goes in v2:
time: 141 us
  Pallas kernels  131 us (93%)
  local copies, waits for them, and re-layouts  8.87 us (6%)
    pallas_call x1, Pallas kernels, per_device(): pl.pallas_call(functools.partial(kernel, (n, tensor, capacity)), out_shap...  131 us
    unnamed x19, local copies, waits for them, and re-layouts  8.87 us

profile of v2, /device:TPU:2, one launch (start us, length us, event | category | flops | bytes accessed | tf_op | source)
XLA Modules:
  0.0 140.6 jit_solution(8252121439348439152)
XLA Ops:
  0.6 0.0 copy-start.6
  0.6 0.0 copy-start.5
  0.7 0.7 copy-done.6
  1.3 0.0 copy-done.5
  1.3 0.0 copy-start
  1.3 1.0 copy-done
  2.3 0.0 copy-start.1
  2.3 1.0 copy-done.1
  3.3 0.0 copy-start.2
  3.3 1.0 copy-done.2
  4.3 0.0 copy-start.3
  4.3 0.9 copy-done.3
  5.2 0.0 copy-start.4
  5.2 0.9 copy-done.4
  6.1 131.0 %shard_map.110 = (bf16[8,192]{1,0:T(8,128)(2,1)S(1)}, bf16[8,192]{1,0:T(8,128)(2,1)S(1)}, bf16[192,1024]{1,0:T(8,128)(2,1)S(1)}, bf16[192,1024]{1,0:T(8,128)(2,1)S(1)}, bf16[192,1024]{1,0:T(8,128)(2,1)S(1)}) custom-call(bf16[8,6144]{1,0:T(8,128)(2,1)S(1)} %copy-done.3, s32[2,8]{1,0:T(2,128)S(1)} %bitcast.26, f32[2,8]{1,0:T(2,128)S(1)} %bitcast.27, ...), custom_call_target="tpu_custom_call" | custom-call | tf_op jit(solution)/shard_map/pallas_call | solution.py:501
  137.1 0.6 copy.17
  137.7 0.6 copy.18
  138.3 0.7 copy.19
  139.1 0.7 copy.20
  139.8 0.7 copy.21
Async XLA Ops:
  0.6 0.7 copy-start.6
  0.6 0.7 copy-start.5
  1.3 1.0 copy-start
  2.3 1.0 copy-start.1
  3.3 1.0 copy-start.2
  4.3 0.9 copy-start.3
  5.2 0.9 copy-start.4

commit v3 on v2

--- a/solution.py
+++ b/solution.py
@@ -94,9 +94,9 @@
 def kernel(
     sizes,
     tok_hbm, ids_hbm, gates_hbm, wg_hbm, wu_hbm, wo_hbm, cot_hbm,
-    mixed_ref, dtok_ref, dg_ref, du_ref, do_ref,
+    mixed_ref, dtok_ref, dg_hbm, du_hbm, do_hbm,
     tok_ref, ids_ref, gates_ref, wg_ref, wu_ref, wo_ref, cot_ref, load_sem,
-    blk, gathered, select, gate_mat, rows_buf, part, packed, near, half_out, half_in, full_out, full_in,
+    dg_ref, du_ref, do_ref, store_sem, places, blk, gathered, select, gate_mat, rows_buf, part, packed, near, half_out, half_in, full_out, full_in,
     acts, wide_acts, terms, outgo, income, last, final,
     swap_sem, plane_send, plane_recv, near_send, near_recv, chain_send, chain_recv,
     ag_send, ag_recv, share_send, share_recv, back_send, back_recv, end_sem,
@@ -120,9 +120,6 @@
             (wg_hbm, wg_ref), (wu_hbm, wu_ref), (wo_hbm, wo_ref),
         ))
     ]
-    for load in loads:
-        load.start()
-
     z = lax.axis_index("dp")
     e = lax.axis_index("expert")
     t = lax.axis_index("tensor")
@@ -146,6 +143,9 @@
     for step in NEIGHBOURS:
         pl.semaphore_signal(barrier, inc=1, device_id=along(step), device_id_type=MESH)
 
+    for load in loads:
+        load.start()
+
     def greet(k, _):
         j = lax.rem(index + k, n)
         pl.semaphore_signal(barrier, inc=1, device_id=peer(j), device_id_type=MESH)
@@ -154,6 +154,13 @@
     lax.fori_loop(1, n, greet, 0)
     for load in loads[:4]:
         load.wait()
+    lines = n * 2 * group
+    line = iota((lines, 2 * rows_n), 0)
+    inner = lax.rem(line, 2 * group)
+    place = capacity * (line // (2 * group)) + jnp.where(inner < group, 0, rows_n)
+    places[...] = (place - iota((lines, 2 * rows_n), 1)).astype(F32)
+    part[:, used:] = jnp.zeros((n, full - used, LANES), F32)
+    full_in[:, used:] = jnp.zeros((leaders - 1, full - used, LANES), F32)
     blk[...] = source_block(index, feats, tok_ref, cot_ref, ids_ref, gates_ref)
     pl.semaphore_wait(barrier, n - 1 + len(NEIGHBOURS) + jnp.where(away, 1, 0))
 
@@ -191,16 +198,11 @@
     lax.fori_loop(1, n, lambda k, _: (spread(k).start(), 0)[1], 0)
     lax.fori_loop(1, n, lambda k, _: (arrival(k).wait_recv(), 0)[1], 0)
 
-    lines = n * 2 * group
     block = gathered[...].reshape(lines, 256)
     meta = block[:, LANES:]
     base = feats - LANES
     pick = (iota((LANES, 2 * rows_n), 0) == base + e).astype(F32).astype(BF16)
-    slot = nn(meta, pick)
-    line = iota((lines, 2 * rows_n), 0)
-    inner = lax.rem(line, 2 * group)
-    place = capacity * (line // (2 * group)) + jnp.where(inner < group, 0, rows_n)
-    sel = (slot + place.astype(F32) == iota((lines, 2 * rows_n), 1).astype(F32)).astype(F32)
+    sel = (nn(meta, pick) + places[...] == 0.0).astype(F32)
     sel = sel.astype(BF16)
     select[...] = sel
     depth = iota((LANES, feats), 0) - base - e
@@ -214,7 +216,6 @@
     rows = rows_all[:rows_n]
     cot_rows = rows_all[rows_n:]
 
-    part[:, used:] = jnp.zeros((n, full - used, LANES), F32)
     for load in loads[4:]:
         load.wait()
     for a, (left_arg, w_ref) in enumerate(
@@ -299,8 +300,6 @@
     def ways(s):
         return ((1, to_right), (-1, to_left)) if s < hops_left else ((1, to_right),)
 
-    if used < full:
-        full_in[:, used:] = jnp.zeros((leaders - 1, full - used, LANES), F32)
     send_near(targets_of(0))
     send_near(targets_of(1))
     for s in range(hops_right):
@@ -436,9 +435,15 @@
     income[index] = outgo[index]
 
     rows_kept = rows_buf[:rows_n]
-    do_ref[...] = tn(rows_buf[rows_n:], hidden_all).astype(BF16)
-    dg_ref[...] = tn(rows_kept, gg_all).astype(BF16)
-    du_ref[...] = tn(rows_kept, gu_all).astype(BF16)
+    stores = []
+    for k, (own, acts_all, buf, out) in enumerate((
+        (rows_buf[rows_n:], hidden_all, do_ref, do_hbm),
+        (rows_kept, gg_all, dg_ref, dg_hbm),
+        (rows_kept, gu_all, du_ref, du_hbm),
+    )):
+        buf[...] = tn(own, acts_all).astype(BF16)
+        stores.append(pltpu.make_async_copy(buf, out, store_sem.at[k]))
+        stores[k].start()
 
     lax.fori_loop(1, n, lambda k, _: (got_back(k).wait_recv(), 0)[1], 0)
     last[...] = jnp.sum(income[...], axis=0).astype(BF16)
@@ -474,6 +479,9 @@
                 chain_copy(way, s, p).wait_send()
                 chain_back(way, s, 0, p).wait_send()
 
+    for store in stores:
+        store.wait()
+
     @pl.when(away)
     def _():
         finish().wait()
@@ -481,6 +489,21 @@
     done = final[...].astype(F32)
     mixed_ref[...] = done[:group].astype(BF16)
     dtok_ref[...] = done[group:].astype(BF16)
+
+
+def hand_out(*refs):
+    count = len(refs) // 3
+    taken, given, held = refs[:count], refs[count : 2 * count], refs[2 * count : 3 * count]
+    in_sem, out_sem = refs[3 * count :]
+    loads = [pltpu.make_async_copy(taken[k], held[k], in_sem.at[k]) for k in range(count)]
+    stores = [pltpu.make_async_copy(held[k], given[k], out_sem.at[k]) for k in range(count)]
+    for load in loads:
+        load.start()
+    for load, store in zip(loads, stores):
+        load.wait()
+        store.start()
+    for store in stores:
+        store.wait()
 
 
 def per_device(n, tensor, experts, tokens, expert_ids, gates, w_gate, w_up, w_out, cotangent):
@@ -498,11 +521,12 @@
     dma = pltpu.SemaphoreType.DMA
     weight = jax.ShapeDtypeStruct((feats, hidden_units), BF16)
     small = jax.ShapeDtypeStruct((group, feats), BF16)
-    mixed, d_tokens, d_gate, d_up, d_out = pl.pallas_call(
+    shapes = (small, small, weight, weight, weight)
+    results = pl.pallas_call(
         functools.partial(kernel, (n, tensor, capacity)),
-        out_shape=(small, small, weight, weight, weight),
+        out_shape=shapes,
         in_specs=[hbm] * 7,
-        out_specs=(vmem,) * 5,
+        out_specs=(vmem, vmem, hbm, hbm, hbm),
         scratch_shapes=[
             pltpu.VMEM(tokens.shape, BF16),
             pltpu.VMEM((2, group), jnp.int32),
@@ -512,6 +536,11 @@
             pltpu.VMEM((feats, hidden_units), BF16),
             pltpu.VMEM(tokens.shape, BF16),
             dma((7,)),
+            pltpu.VMEM((feats, hidden_units), BF16),
+            pltpu.VMEM((feats, hidden_units), BF16),
+            pltpu.VMEM((feats, hidden_units), BF16),
+            dma((3,)),
+            pltpu.VMEM((n * 2 * group, 2 * rows_n), F32),
             pltpu.VMEM((2 * group, 256), BF16),
             pltpu.VMEM((n, 2 * group, 256), BF16),
             pltpu.VMEM((n * 2 * group, 2 * rows_n), BF16),
@@ -547,11 +576,19 @@
             dma((2,)),
         ],
         compiler_params=pltpu.CompilerParams(
-            collective_id=0, has_side_effects=True, vmem_limit_bytes=40 * 1024 * 1024
+            collective_id=0, has_side_effects=True, vmem_limit_bytes=60 * 1024 * 1024
         ),
     )(
         tokens, expert_ids.T, gates.T, w_gate[0].T, w_up[0].T, w_out[0].T, cotangent
     )
+    mixed, d_tokens, d_gate, d_up, d_out = pl.pallas_call(
+        hand_out,
+        out_shape=shapes,
+        in_specs=[hbm] * 5,
+        out_specs=(hbm,) * 5,
+        scratch_shapes=[pltpu.VMEM(v.shape, BF16) for v in shapes] + [dma((5,)), dma((5,))],
+        compiler_params=pltpu.CompilerParams(vmem_limit_bytes=60 * 1024 * 1024),
+    )(*results)
     return (mixed, d_tokens, d_gate.T[None], d_up.T[None], d_out.T[None])
 
 

time: 141 us -> 134 us (0.950)
  local copies, waits for them, and re-layouts: 8.87 us -> 0 us
  Pallas kernels: 131 us -> 133 us
    unnamed x19 -> x0, local copies, waits for them, and re-layouts: 8.87 us -> none
    pallas_call x0 -> x1, Pallas kernels: none -> 2.1 us  [per_device(): pl.pallas_call(hand_out, out_shape=shapes, in_specs=[hbm] * 5, out_specs=...]
where the time goes in v3:
time: 134 us
  Pallas kernels  133 us (99%)
    pallas_call x1, Pallas kernels, per_device(): pl.pallas_call(functools.partial(kernel, (n, tensor, capacity)), out_shap...  131 us

profile of v3, /device:TPU:2, one launch (start us, length us, event | category | flops | bytes accessed | tf_op | source)
XLA Modules:
  0.0 134.1 jit_solution(8970632822059220892)
XLA Ops:
  0.6 131.4 %shard_map.110 = (bf16[8,192]{1,0:T(8,128)(2,1)}, bf16[8,192]{1,0:T(8,128)(2,1)}, bf16[192,1024]{1,0:T(8,128)(2,1)}, bf16[192,1024]{1,0:T(8,128)(2,1)}, bf16[192,1024]{1,0:T(8,128)(2,1)}) custom-call(bf16[8,6144]{1,0:T(8,128)(2,1)} %tok_hbm.1, s32[2,8]{1,0:T(2,128)} %bitcast.23, f32[2,8]{1,0:T(2,128)} %bitcast.24, bf16[192,1024]{1,0:T(8,128)(2,1)} %bitcast.20, ...), custom_call_target="tpu_custom_call" | custom-call | tf_op jit(solution)/shard_map/pallas_call | solution.py:525
  132.0 2.1 %shard_map.111 = (bf16[8,192]{1,0:T(8,128)(2,1)}, bf16[8,192]{1,0:T(8,128)(2,1)}, bf16[192,1024]{1,0:T(8,128)(2,1)}, bf16[192,1024]{1,0:T(8,128)(2,1)}, bf16[192,1024]{1,0:T(8,128)(2,1)}) custom-call(bf16[8,192]{1,0:T(8,128)(2,1)} %get-tuple-element.15.refs_0_, bf16[8,192]{1,0:T(8,128)(2,1)} %get-tuple-element.16.refs_1_, ...), custom_call_target="tpu_custom_call" | custom-call | tf_op jit(solution)/shard_map/pallas_call | solution.py:584
